TPU v7x, 32 devices: a whole 2x2x4 slice. The times are simulated.
32 devices in a mesh: groups: 2 (over y), cache: 4 (over z), blk: 4 (over x, core).
Axes of the slice: x: 2, y: 2, z: 4, core: 2. Of those that a mesh axis runs over, the one named last changes fastest.
Arguments:
- queries: bfloat16 [8, 512, 2048], P(('groups', 'cache'), 'blk'), parts along dimension 0, may hold values from -6 to 6
- kv_new: bfloat16 [8, 512, 1024], P(('groups', 'cache'), 'blk'), parts along dimension 0, may hold values from -6 to 6
- page_pool: bfloat16 [8, 128, 8, 1024], P(('groups', 'cache')), parts along dimension 0, may hold values from -6 to 6
- page_owner: int32 [8, 4, 32, 1], P(('groups', 'cache'), 'blk'), parts along dimension 0, may hold values from 0 to 3; in each aligned block of 32 rows (0 to 31, 32 to 63, ..., all dimensions but the last counted through in order) at most 16 rows name the same one
- page_slot: int32 [8, 4, 32], P(('groups', 'cache'), 'blk'), parts along dimension 0, may hold values from 0 to 127
- prefix_len: int32 [8], P(('groups', 'cache')), parts along dimension 0, may hold values from 1 to 1024, 2048 in all
- suffix_len: int32 [8], P(('groups', 'cache')), parts along dimension 0, may hold values from 1 to 512, 1536 in all
- ssm_in: bfloat16 [8, 512, 2048], P(('groups', 'cache'), 'blk'), parts along dimension 0, may hold values from -6 to 6
- b_in: bfloat16 [8, 512, 128], P(('groups', 'cache'), 'blk'), parts along dimension 0, may hold values from -4 to 4
- c_in: bfloat16 [8, 512, 128], P(('groups', 'cache'), 'blk'), parts along dimension 0, may hold values from -4 to 4
- step_size: float32 [8, 512, 32], P(('groups', 'cache'), 'blk'), parts along dimension 0, may hold values from 0.01 to 0.1
- decay_rate: float32 [32], replicated, may hold values from 0.001953125 to 4
- skip_gain: float32 [32], replicated, may hold values from 0.5 to 1.5
- prior_state: float32 [8, 32, 64, 128], P(('groups', 'cache')), parts along dimension 0, may hold values from -4 to 4
Outputs:
- attn_out: bfloat16 [8, 512, 2048], P(('groups', 'cache'), 'blk'), parts along dimension 0
- ssm_out: bfloat16 [8, 512, 2048], P(('groups', 'cache'), 'blk'), parts along dimension 0
There are 2 independent parts, one for each index of `groups`. A program takes and returns all parts, laid end to end along the dimension named above; an argument that names none is the same for every part. Nothing has to cross between parts.
Inputs may be any that keep to these rules, and one draw needn't show every extreme that they name: `page_owner`: among the 32 pages of one request at one index of blk, no owner is named more than 16 times, a bound that some block reaches. `prefix_len`: the largest is 1024. `suffix_len`: the largest is 512.
All inputs are finite; a program needn't handle non-finite values. No bound on the sum of `prefix_len` or of `suffix_len` on one device may be relied on, other than what follows from the above.
Results may differ from a plain program's by a relative error of at most 0.008.
Values may be sent and summed in bfloat16 or wider, within the bound.
A program may use at most 128 MiB of HBM per device.

v0:
```python
import math
import jax
import jax.numpy as jnp
from jax import lax
from jax.sharding import PartitionSpec as P

QH = 16
KVH = 4
HD = 128
SH = 32
HP = 64
NS = 128
PAGE = 8
LIST = 32
NEG = -1e30


def passed_along(value, axis, steps):
    count = lax.axis_size(axis)
    leading, last = (max(0, -steps), min(count, count - steps))
    return lax.ppermute(value, axis, [(source, source + steps) for source in range(leading, last)])


def for_sending(shard):

    def short(part):
        return part.astype(jnp.bfloat16) if part.dtype == jnp.float32 else part

    return jax.tree.map(short, shard)


def attend(carry, grouped, block_rows, visible):
    biggest, totals, accum = carry
    count = block_rows.shape[0]
    half = block_rows.shape[1] // 2
    keys_part = block_rows[:, :half].reshape(count, KVH, HD)
    values_part = block_rows[:, half:].reshape(count, KVH, HD)
    scores = jnp.einsum(
        "qhgd,khd->hgqk", grouped, keys_part, preferred_element_type=jnp.float32
    ) * (1.0 / math.sqrt(HD))
    masked = jnp.where(visible[None, None], scores, NEG)
    renewed = jnp.maximum(biggest, jnp.max(masked, axis=-1))
    weights = jnp.where(visible[None, None], jnp.exp(scores - renewed[..., None]), 0.0)
    factor = jnp.exp(biggest - renewed)
    totals = totals * factor + jnp.sum(weights, axis=-1)
    accum = accum * factor[..., None] + jnp.einsum(
        "hgqk,khd->hgqd",
        weights.astype(jnp.bfloat16),
        values_part,
        preferred_element_type=jnp.float32,
    )
    return (renewed, totals, accum)


def fetch_pages(owner_list, slot_list, pool_pages, capacity):
    owners_count = lax.axis_size("cache")
    onehot = (owner_list[:, None] == jnp.arange(owners_count, dtype=jnp.int32)[None, :]).astype(
        jnp.int32
    )
    earlier = jnp.cumsum(onehot, axis=0) - onehot
    ranking = jnp.sum(earlier * onehot, axis=1)
    wanted_slots = (
        jnp.zeros((owners_count, capacity), jnp.int32).at[owner_list, ranking].set(slot_list)
    )
    arrived = lax.all_to_all(
        pool_pages[lax.all_to_all(wanted_slots, "cache", split_axis=0, concat_axis=0, tiled=True)],
        "cache",
        split_axis=0,
        concat_axis=0,
        tiled=True,
    )
    return arrived[owner_list, ranking]


def combine(earlier, later):
    return (earlier[0] * later[0], later[0][:, None, None] * earlier[1] + later[1])


def local(
    queries,
    kv_new,
    page_pool,
    page_owner,
    page_slot,
    prefix_len,
    suffix_len,
    ssm_in,
    b_in,
    c_in,
    step_size,
    decay_rate,
    skip_gain,
    prior_state,
):
    blocks = lax.axis_size("blk")
    position_here = lax.axis_index("blk")
    tokens = queries.shape[1]
    kv_width = kv_new.shape[2]
    group = QH // KVH
    prefix_limit = prefix_len[0]
    suffix_limit = suffix_len[0]
    local_positions = jnp.arange(tokens, dtype=jnp.int32)
    query_positions = position_here * tokens + local_positions
    grouped = queries[0].reshape(tokens, KVH, group, HD)
    carry = (
        jnp.full((KVH, group, tokens), NEG, jnp.float32),
        jnp.zeros((KVH, group, tokens), jnp.float32),
        jnp.zeros((KVH, group, tokens, HD), jnp.float32),
    )
    pool_pages = page_pool[0]
    capacity = max(2, 2 * LIST // lax.axis_size("cache"))
    all_owners, all_slots = (
        lax.all_gather(page_owner[:, :, :, 0], "blk", axis=1, tiled=True),
        lax.all_gather(page_slot, "blk", axis=1, tiled=True),
    )
    fetched = fetch_pages(
        all_owners[0].reshape(-1), all_slots[0].reshape(-1), pool_pages, capacity * blocks
    )
    page_rows = fetched.reshape(-1, kv_width)
    block_ids = jnp.arange(blocks, dtype=jnp.int32)[:, None, None]
    item_ids = jnp.arange(LIST, dtype=jnp.int32)[None, :, None]
    offsets = jnp.arange(PAGE, dtype=jnp.int32)[None, None, :]
    page_positions = ((item_ids * blocks + block_ids) * PAGE + offsets).reshape(-1)
    valid = page_positions < prefix_limit
    total = page_rows.shape[0]
    width = 512

    def page_block(index, state):
        rows_block = lax.dynamic_slice_in_dim(page_rows, index * width, width, 0)
        seen = lax.dynamic_slice_in_dim(valid, index * width, width, 0)
        return attend(state, grouped, rows_block, jnp.broadcast_to(seen[None, :], (tokens, width)))

    carry = lax.fori_loop(0, total // width, page_block, carry)
    suffix_rows = kv_new[0]
    for step in range(blocks):
        if step > 0:
            suffix_rows = passed_along(suffix_rows, "blk", 1)
        anchor = (position_here - step) % blocks
        key_positions = anchor * tokens + local_positions
        carry = attend(
            carry,
            grouped,
            suffix_rows,
            (key_positions[None, :] <= query_positions[:, None])
            & (key_positions[None, :] < suffix_limit),
        )
    biggest, totals, accum = carry
    mixed = jnp.transpose(accum / totals[..., None], (2, 0, 1, 3)).reshape(tokens, QH * HD)
    attn_out = jnp.where((query_positions < suffix_limit)[:, None], mixed, 0.0).astype(
        jnp.bfloat16
    )[None]
    inputs = ssm_in[0].reshape(tokens, SH, HP)
    b_rows = b_in[0]
    c_rows = c_in[0]
    steps_dt = step_size[0]
    logs = jnp.cumsum(-steps_dt * decay_rate[None, :], axis=0)
    last = logs[-1]
    gram = jnp.dot(c_rows, b_rows.T, preferred_element_type=jnp.float32)
    lower = local_positions[:, None] >= local_positions[None, :]
    exponent = jnp.where(lower[None], logs.T[:, :, None] - logs.T[:, None, :], NEG)
    mixing = (gram[None] * jnp.exp(exponent) * steps_dt.T[:, None, :]).astype(jnp.bfloat16)
    inner = jnp.einsum("hts,shp->thp", mixing, inputs, preferred_element_type=jnp.float32)
    scaled = (
        (jnp.exp(last[None, :] - logs) * steps_dt)[:, :, None] * inputs.astype(jnp.float32)
    ).astype(jnp.bfloat16)
    local_state = jnp.einsum("shp,sn->hpn", scaled, b_rows, preferred_element_type=jnp.float32)
    local_decay = jnp.exp(last)
    identity = (jnp.ones((SH,), jnp.float32), jnp.zeros((SH, HP, NS), jnp.float32))
    prefix_decay, prefix_state = identity
    for round_index in range(blocks - 1):
        outgoing = combine((prefix_decay, prefix_state), (local_decay, local_state))
        incoming = passed_along((for_sending(outgoing[0]), for_sending(outgoing[1])), "blk", 1)
        prefix_decay = jnp.where(position_here == 0, identity[0], incoming[0])
        prefix_state = jnp.where(position_here == 0, identity[1], incoming[1])
    entering = prefix_decay[:, None, None] * prior_state[0] + prefix_state
    carried = jnp.exp(logs)[:, :, None] * jnp.einsum(
        "tn,hpn->thp", c_rows.astype(jnp.float32), entering, precision=lax.Precision.HIGHEST
    )
    result = inner + carried + skip_gain[None, :, None] * inputs.astype(jnp.float32)
    result = jnp.where((query_positions < suffix_limit)[:, None, None], result, 0.0)
    ssm_out = result.reshape(tokens, SH * HP).astype(jnp.bfloat16)[None]
    return (attn_out, ssm_out)


def solution(mesh):
    in_specs = (
        P(("groups", "cache"), "blk", None),
        P(("groups", "cache"), "blk", None),
        P(("groups", "cache"), None, None, None),
        P(("groups", "cache"), "blk", None, None),
        P(("groups", "cache"), "blk", None),
        P(("groups", "cache")),
        P(("groups", "cache")),
        P(("groups", "cache"), "blk", None),
        P(("groups", "cache"), "blk", None),
        P(("groups", "cache"), "blk", None),
        P(("groups", "cache"), "blk", None),
        P(),
        P(),
        P(("groups", "cache"), None, None, None),
    )
    out_specs = (P(("groups", "cache"), "blk", None), P(("groups", "cache"), "blk", None))
    return jax.shard_map(local, mesh=mesh, in_specs=in_specs, out_specs=out_specs, check_vma=False)
```

profile of v0, /device:TPU:0, one launch (start us, length us, event | category | flops | bytes accessed | tf_op | source)
XLA Modules:
  0.0 198.7 jit_solution(4039296911272048753)
XLA Ops:
  0.6 6.3 %all-gather = s32[1,4,32,1]{2,3,0,1:T(1,128)S(1)} all-gather(s32[1,1,32,1]{2,3,0,1:T(1,128)} %bitcast.279), channel_id=2, replica_groups=mesh['groups'=2,'cache'=4,'blk'=4] {'blk'}, dimensions={1}, use_global_device_ids=true | all-gather | bytes 640 | tf_op jit(solution)/shard_map/all_gather | solution.py:113
  8.7 5.4 %all_gather.7 = s32[1,4,32]{2,0,1:T(1,128)S(1)} all-gather(s32[1,1,32]{2,0,1:T(1,128)} %bitcast.280), channel_id=1, replica_groups=mesh['groups'=2,'cache'=4,'blk'=4] {'blk'}, dimensions={1}, use_global_device_ids=true | all-gather | bytes 640 | tf_op jit(solution)/shard_map/all_gather | solution.py:114
  15.4 19.7 %scatter_fusion = s32[4,64]{1,0:T(4,128)} fusion(s32[4,64]{1,0:T(4,128)} %broadcast.351, s32[128]{0:T(128)S(1)} %get-tuple-element.209, s32[128]{0:T(128)S(1)} %reshape.502), kind=kCustom, calls=%fused_computation.2 | custom fusion | bytes 2560 | tf_op jit(solution)/shard_map/scatter | solution.py:63
  35.1 5.1 %all-to-all-start = ((s32[4,1,64]{2,1,0:T(1,128)}), s32[4,1,64]{2,1,0:T(1,128)S(1)}, u32[]{:S(2)}, u32[]{:S(2)}) async-start(s32[4,1,64]{2,1,0:T(1,128)} %bitcast.8), calls=%async_computation | async-start | bytes 4096 | tf_op jit(solution)/shard_map/all_to_all | solution.py:66
  46.3 3.3 %collective-permute-start.3 = (bf16[32]{0:T(256)(128)(2,1)}, bf16[32]{0:T(256)(128)(2,1)}, u32[]{:S(2)}, u32[]{:S(2)}) collective-permute-start(bf16[32]{0:T(256)(128)(2,1)} %fusion.89), channel_id=1, source_target_pairs={{0,1},{1,2},{2,3},{4,5},{5,6},{6,7},{8,9},{9,10},{10,11},{12,13},{... | collective-permute-start | bytes 200 | tf_op jit(solution)/shard_map/ppermute | solution.py:21
  49.7 2.8 %gather_fusion = bf16[256,8,1024]{2,1,0:T(8,128)(2,1)} fusion(bf16[128,8,1024]{2,1,0:T(8,128)(2,1)S(1)} %bitcast.226, s32[1024]{0:T(1024)S(1)} %pad_clamp_fusion), kind=kCustom, calls=%fused_computation | custom fusion | bytes 8389632 | tf_op jit(solution)/shard_map/gather | solution.py:66
  52.5 5.2 %all-to-all-start.1 = ((bf16[4,64,8,1024]{3,2,1,0:T(8,128)(2,1)}), bf16[4,64,8,1024]{3,2,1,0:T(8,128)(2,1)}, u32[]{:S(2)}, u32[]{:S(2)}) async-start(bf16[4,64,8,1024]{3,2,1,0:T(8,128)(2,1)} %bitcast.234), calls=%async_computation.1 | async-start | bytes 8388608 | tf_op jit(solution)/shard_map/all_to_all | solution.py:65
  65.7 2.7 %convolution_bitcast_fusion.1 = f32[128,32,64]{0,2,1:T(8,128)} fusion(bf16[128,32,64]{0,2,1:T(8,128)(2,1)S(1)} %bitcast.237, f32[32,128]{1,0:T(8,128)} %bitcast.276, f32[32,128]{1,0:T(8,128)} %copy.119, f32[128,128]{1,0:T(8,128)S(1)} %fusion.73, pred[128,128]{1,0:T(8,128)(4,1)S(1)} %iota_compare_fusion), kind=kOutput, calls=%fused_computation.46 | convolution fusion | flops 69730304 | bytes 1687552 | tf_op jit(solution)/shard_map/hts,shp->thp/dot_general | solution.py:162
  75.5 3.0 %collective-permute-start.6 = (bf16[32,64,128]{2,1,0:T(8,128)(2,1)}, bf16[32,64,128]{2,1,0:T(8,128)(2,1)}, u32[]{:S(2)}, u32[]{:S(2)}) collective-permute-start(bf16[32,64,128]{2,1,0:T(8,128)(2,1)} %get-tuple-element.240), channel_id=1, source_target_pairs={{0,1},{1,2},{2,3},{4,5},{5,6},{6,7},{8,9},{9,10},{10,11},{12,13},{... | collective-permute-start | bytes 1572872 | tf_op jit(solution)/shard_map/ppermute | solution.py:21
  80.3 3.1 %collective-permute-start.5 = (bf16[32]{0:T(256)(128)(2,1)S(1)}, bf16[32]{0:T(256)(128)(2,1)S(1)}, u32[]{:S(2)}, u32[]{:S(2)}) collective-permute-start(bf16[32]{0:T(256)(128)(2,1)S(1)} %get-tuple-element.225), channel_id=1, source_target_pairs={{0,1},{1,2},{2,3},{4,5},{5,6},{6,7},{8,9},{9,10},{10,11},{12,13},{... | collective-permute-start | bytes 200 | tf_op jit(solution)/shard_map/ppermute | solution.py:21
  85.0 3.1 %collective-permute-start.1 = (bf16[128,1024]{0,1:T(8,128)(2,1)}, bf16[128,1024]{0,1:T(8,128)(2,1)S(1)}, u32[]{:S(2)}, u32[]{:S(2)}) collective-permute-start(bf16[128,1024]{0,1:T(8,128)(2,1)} %collective-permute-done), channel_id=1, source_target_pairs={{0,1},{1,2},{2,3},{4,5},{5,6},{6,7},{8,9},{9,10},{10,11},{12,13},{... | collective-permute-start | bytes 786440 | tf_op jit(solution)/shard_map/ppermute | solution.py:21
  89.6 4.4 %collective-permute-start.7 = (bf16[32,64,128]{2,1,0:T(8,128)(2,1)S(1)}, bf16[32,64,128]{2,1,0:T(8,128)(2,1)S(1)}, u32[]{:S(2)}, u32[]{:S(2)}) collective-permute-start(bf16[32,64,128]{2,1,0:T(8,128)(2,1)S(1)} %add_convert_fusion.1), channel_id=1, source_target_pairs={{0,1},{1,2},{2,3},{4,5},{5,6},{6,7},{8,9},{9,10},{10,11},{12,13},{... | collective-permute-start | bytes 1572872 | tf_op jit(solution)/shard_map/ppermute | solution.py:21
  99.8 3.2 %collective-permute-start.8 = (bf16[32,64,128]{2,1,0:T(8,128)(2,1)S(1)}, bf16[32,64,128]{2,1,0:T(8,128)(2,1)S(1)}, u32[]{:S(2)}, u32[]{:S(2)}) collective-permute-start(bf16[32,64,128]{2,1,0:T(8,128)(2,1)S(1)} %add_convert_fusion), channel_id=1, source_target_pairs={{0,1},{1,2},{2,3},{4,5},{5,6},{6,7},{8,9},{9,10},{10,11},{12,13},{... | collective-permute-start | bytes 1572872 | tf_op jit(solution)/shard_map/ppermute | solution.py:21
  103.0 2.6 %select_reduce_fusion.1 = (f32[4,4,128]{2,1,0:T(4,128)}, f32[4,4,128,128]{2,3,1,0:T(8,128)}) fusion(pred[128,128]{0,1:T(8,128)(4,1)} %get-tuple-element.229, bf16[128,4,128,1]{0,2,3,1:T(8,128)(2,1)S(1)} %bitcast.250, bf16[128,4,4,128]{0,3,2,1:T(8,128)(2,1)S(1)} %bitcast.232), kind=kOutput, calls=%fused_computation.66 | convolution fusion | flops 67893248 | bytes 1728512 | tf_op jit(solution)/shard_map/qhgd,khd->hgqk/dot_general | solution.py:38
  110.3 40.6 %all-to-all-done.1 = bf16[4,64,8,1024]{3,2,1,0:T(8,128)(2,1)} async-done(((bf16[4,64,8,1024]{3,2,1,0:T(8,128)(2,1)}), bf16[4,64,8,1024]{3,2,1,0:T(8,128)(2,1)}, u32[]{:S(2)}, u32[]{:S(2)}) %all-to-all-start.1) | async-done | bytes 4194336 | tf_op jit(solution)/shard_map/all_to_all | solution.py:65
  150.9 4.4 %gather_fusion.1 = bf16[128,8,1024]{2,1,0:T(8,128)(2,1)} fusion(bf16[4,64,8,1024]{3,2,1,0:T(8,128)(2,1)} %all-to-all-done.1, s32[128]{0:T(128)S(1)} %bitcast.236), kind=kCustom, calls=%fused_computation.1 | custom fusion | bytes 4195328 | tf_op jit(solution)/shard_map/gather | solution.py:72
  155.3 31.0 %while.18 = (s32[]{:T(128)}, f32[4,4,128]{2,1,0:T(4,128)S(1)}, f32[4,4,128]{2,1,0:T(4,128)}, f32[4,4,128,128]{3,2,1,0:T(8,128)}, pred[1024]{0:T(1024)(128)(4,1)S...) while((s32[]{:T(128)}, f32[4,4,128]{2,1,0:T(4,128)S(1)}, ...), condition=%wide.region_6.7_spmd.clone, body=%wide.region_3.6_spmd.clone.sunk | while | flops 549201920 | bytes 20581072 | solution.py:133
  157.7 4.2 %fusion.129 = (f32[4,4,128]{2,1,0:T(4,128)S(1)}, f32[4,512,128,4]{2,1,3,0:T(8,128)}) fusion(pred[512]{0:T(512)(128)(4,1)S(1)} %dynamic_slice.17, bf16[512,4,128,1]{0,2,3,1:T(8,128)(2,1)} %bitcast.227, bf16[128,4,4,128]{3,0,2,1:T(8,128)(2,1)} %get-tuple-element.344), kind=kOutput, calls=%fused_computation.5.clone.1 | convolution fusion | flops 271579136 | bytes 5251584 | tf_op jit(solution)/shard_map/while/body/eval_jaxpr/qhgd,khd->hgqk/dot_general | solution.py:38
  161.9 3.1 %fusion.130 = f32[4,4,128]{2,1,0:T(4,128)S(1)} fusion(f32[4,512,128,4]{2,1,3,0:T(8,128)} %get-tuple-element.310, f32[4,4,128]{2,1,0:T(4,128)S(1)} %select_maximum_fusion.2, pred[512]{0:T(512)(128)(4,1)S(1)} %dynamic_slice.17), kind=kLoop, calls=%fused_computation.9.clone.1 | loop fusion | flops 4192256 | bytes 4211200 | tf_op jit(solution)/shard_map/while/body/eval_jaxpr/reduce_sum | solution.py:45
  165.8 4.5 %fusion.132 = f32[4,4,128,128]{3,2,1,0:T(8,128)} fusion(bf16[512,4,128,1]{0,2,3,1:T(8,128)(2,1)S(1)} %bitcast.235, f32[4,512,128,4]{2,1,3,0:T(8,128)} %get-tuple-element.310, f32[4,4,128]{2,1,0:T(4,128)S(1)} %select_maximum_fusion.2, pred[512]{0:T(512)(128)(4,1)S(1)} %dynamic_slice.17, f32[4,4,128,128]{3,2,1,0:T(8,128)} %get-tuple-element.329, ...), kind=kOutput, calls=%fused_computation.15.clone.1 | convolution fusion | flops 273416192 | bytes 6832641 | tf_op jit(solution)/shard_map/while/body/eval_jaxpr/hgqk,khd->hgqd/dot_general | solution.py:46
  172.7 4.2 %fusion.129 = (f32[4,4,128]{2,1,0:T(4,128)S(1)}, f32[4,512,128,4]{2,1,3,0:T(8,128)}) fusion(pred[512]{0:T(512)(128)(4,1)S(1)} %dynamic_slice.17, bf16[512,4,128,1]{0,2,3,1:T(8,128)(2,1)} %bitcast.227, bf16[128,4,4,128]{3,0,2,1:T(8,128)(2,1)} %get-tuple-element.344), kind=kOutput, calls=%fused_computation.5.clone.1 | convolution fusion | flops 271579136 | bytes 5251584 | tf_op jit(solution)/shard_map/while/body/eval_jaxpr/qhgd,khd->hgqk/dot_general | solution.py:38
  176.9 3.1 %fusion.130 = f32[4,4,128]{2,1,0:T(4,128)S(1)} fusion(f32[4,512,128,4]{2,1,3,0:T(8,128)} %get-tuple-element.310, f32[4,4,128]{2,1,0:T(4,128)S(1)} %select_maximum_fusion.2, pred[512]{0:T(512)(128)(4,1)S(1)} %dynamic_slice.17), kind=kLoop, calls=%fused_computation.9.clone.1 | loop fusion | flops 4192256 | bytes 4211200 | tf_op jit(solution)/shard_map/while/body/eval_jaxpr/reduce_sum | solution.py:45
  181.5 4.8 %fusion.132 = f32[4,4,128,128]{3,2,1,0:T(8,128)} fusion(bf16[512,4,128,1]{0,2,3,1:T(8,128)(2,1)S(1)} %bitcast.235, f32[4,512,128,4]{2,1,3,0:T(8,128)} %get-tuple-element.310, f32[4,4,128]{2,1,0:T(4,128)S(1)} %select_maximum_fusion.2, pred[512]{0:T(512)(128)(4,1)S(1)} %dynamic_slice.17, f32[4,4,128,128]{3,2,1,0:T(8,128)} %get-tuple-element.329, ...), kind=kOutput, calls=%fused_computation.15.clone.1 | convolution fusion | flops 273416192 | bytes 6832641 | tf_op jit(solution)/shard_map/while/body/eval_jaxpr/hgqk,khd->hgqd/dot_general | solution.py:46
  186.3 2.7 %copy.106 = f32[4,4,128,128]{2,3,1,0:T(8,128)} copy(f32[4,4,128,128]{3,2,1,0:T(8,128)} %get-tuple-element.128) | data formatting | bytes 2097152 | tf_op jit(solution)/shard_map/while | solution.py:133
  (152 shorter events, 54.7 us)
Async XLA Ops:
  0.6 49.0 %copy-start = (bf16[1,128,8,1024]{3,2,1,0:T(8,128)(2,1)S(1)}, bf16[1,128,8,1024]{3,2,1,0:T(8,128)(2,1)}, u32[]{:S(2)}) copy-start(bf16[1,128,8,1024]{3,2,1,0:T(8,128)(2,1)} %param.18) | copy-start | bytes 6291460
  35.1 14.4 %all-to-all-start = ((s32[4,1,64]{2,1,0:T(1,128)}), s32[4,1,64]{2,1,0:T(1,128)S(1)}, u32[]{:S(2)}, u32[]{:S(2)}) async-start(s32[4,1,64]{2,1,0:T(1,128)} %bitcast.8), calls=%async_computation | async-start | bytes 4096 | tf_op jit(solution)/shard_map/all_to_all | solution.py:66
  41.4 43.6 %collective-permute-start = (bf16[128,1024]{0,1:T(8,128)(2,1)S(1)}, bf16[128,1024]{0,1:T(8,128)(2,1)}, u32[]{:S(2)}, u32[]{:S(2)}) collective-permute-start(bf16[128,1024]{0,1:T(8,128)(2,1)S(1)} %bitcast.243), channel_id=1, source_target_pairs={{0,1},{1,2},{2,3},{4,5},{5,6},{6,7},{8,9},{9,10},{10,11},{12,13},{... | collective-permute-start | bytes 786440 | tf_op jit(solution)/shard_map/ppermute | solution.py:21
  46.3 25.0 %collective-permute-start.3 = (bf16[32]{0:T(256)(128)(2,1)}, bf16[32]{0:T(256)(128)(2,1)}, u32[]{:S(2)}, u32[]{:S(2)}) collective-permute-start(bf16[32]{0:T(256)(128)(2,1)} %fusion.89), channel_id=1, source_target_pairs={{0,1},{1,2},{2,3},{4,5},{5,6},{6,7},{8,9},{9,10},{10,11},{12,13},{... | collective-permute-start | bytes 200 | tf_op jit(solution)/shard_map/ppermute | solution.py:21
  52.5 98.4 %all-to-all-start.1 = ((bf16[4,64,8,1024]{3,2,1,0:T(8,128)(2,1)}), bf16[4,64,8,1024]{3,2,1,0:T(8,128)(2,1)}, u32[]{:S(2)}, u32[]{:S(2)}) async-start(bf16[4,64,8,1024]{3,2,1,0:T(8,128)(2,1)} %bitcast.234), calls=%async_computation.1 | async-start | bytes 8388608 | tf_op jit(solution)/shard_map/all_to_all | solution.py:65
  68.4 26.7 %copy-start.12 = (pred[128,128]{0,1:T(8,128)(4,1)S(1)}, pred[128,128]{0,1:T(8,128)(4,1)}, u32[]{:S(2)}) copy-start(pred[128,128]{0,1:T(8,128)(4,1)} %get-tuple-element.231) | copy-start | bytes 49156
  71.9 2.1 %collective-permute-start.4 = (bf16[32]{0:T(256)(128)(2,1)S(1)}, bf16[32]{0:T(256)(128)(2,1)S(1)}, u32[]{:S(2)}, u32[]{:S(2)}) collective-permute-start(bf16[32]{0:T(256)(128)(2,1)S(1)} %fusion.78), channel_id=1, source_target_pairs={{0,1},{1,2},{2,3},{4,5},{5,6},{6,7},{8,9},{9,10},{10,11},{12,13},{... | collective-permute-start | bytes 200 | tf_op jit(solution)/shard_map/ppermute | solution.py:21
  74.0 23.0 %copy-start.22 = (f32[32]{0:T(128)}, f32[32]{0:T(128)S(1)}, u32[]{:S(2)}) copy-start(f32[32]{0:T(128)S(1)} %get-tuple-element.227) | copy-start | bytes 388
  75.5 12.6 %collective-permute-start.6 = (bf16[32,64,128]{2,1,0:T(8,128)(2,1)}, bf16[32,64,128]{2,1,0:T(8,128)(2,1)}, u32[]{:S(2)}, u32[]{:S(2)}) collective-permute-start(bf16[32,64,128]{2,1,0:T(8,128)(2,1)} %get-tuple-element.240), channel_id=1, source_target_pairs={{0,1},{1,2},{2,3},{4,5},{5,6},{6,7},{8,9},{9,10},{10,11},{12,13},{... | collective-permute-start | bytes 1572872 | tf_op jit(solution)/shard_map/ppermute | solution.py:21
  78.6 29.7 %copy-start.23 = (pred[128]{0:T(512)(128)(4,1)}, pred[128]{0:T(512)(128)(4,1)S(1)}, u32[]{:S(2)}) copy-start(pred[128]{0:T(512)(128)(4,1)S(1)} %broadcast_compare_fusion.4) | copy-start | bytes 388
  80.3 4.6 %collective-permute-start.5 = (bf16[32]{0:T(256)(128)(2,1)S(1)}, bf16[32]{0:T(256)(128)(2,1)S(1)}, u32[]{:S(2)}, u32[]{:S(2)}) collective-permute-start(bf16[32]{0:T(256)(128)(2,1)S(1)} %get-tuple-element.225), channel_id=1, source_target_pairs={{0,1},{1,2},{2,3},{4,5},{5,6},{6,7},{8,9},{9,10},{10,11},{12,13},{... | collective-permute-start | bytes 200 | tf_op jit(solution)/shard_map/ppermute | solution.py:21
  84.9 14.0 %copy-start.4 = (f32[32,64,128]{2,1,0:T(8,128)S(1)}, f32[32,64,128]{2,1,0:T(8,128)}, u32[]{:S(2)}) copy-start(f32[32,64,128]{2,1,0:T(8,128)} %get-tuple-element.241) | copy-start | bytes 3145732
  85.0 12.1 %collective-permute-start.1 = (bf16[128,1024]{0,1:T(8,128)(2,1)}, bf16[128,1024]{0,1:T(8,128)(2,1)S(1)}, u32[]{:S(2)}, u32[]{:S(2)}) collective-permute-start(bf16[128,1024]{0,1:T(8,128)(2,1)} %collective-permute-done), channel_id=1, source_target_pairs={{0,1},{1,2},{2,3},{4,5},{5,6},{6,7},{8,9},{9,10},{10,11},{12,13},{... | collective-permute-start | bytes 786440 | tf_op jit(solution)/shard_map/ppermute | solution.py:21
  88.0 18.3 %copy-start.16 = (pred[128,128]{0,1:T(8,128)(4,1)S(1)}, pred[128,128]{0,1:T(8,128)(4,1)}, u32[]{:S(2)}) copy-start(pred[128,128]{0,1:T(8,128)(4,1)} %get-tuple-element.230) | copy-start | bytes 49156
  89.6 9.4 %collective-permute-start.7 = (bf16[32,64,128]{2,1,0:T(8,128)(2,1)S(1)}, bf16[32,64,128]{2,1,0:T(8,128)(2,1)S(1)}, u32[]{:S(2)}, u32[]{:S(2)}) collective-permute-start(bf16[32,64,128]{2,1,0:T(8,128)(2,1)S(1)} %add_convert_fusion.1), channel_id=1, source_target_pairs={{0,1},{1,2},{2,3},{4,5},{5,6},{6,7},{8,9},{9,10},{10,11},{12,13},{... | collective-permute-start | bytes 1572872 | tf_op jit(solution)/shard_map/ppermute | solution.py:21
  95.0 13.3 %copy-start.7 = (f32[1,32,64,128]{3,2,1,0:T(8,128)S(1)}, f32[1,32,64,128]{3,2,1,0:T(8,128)}, u32[]{:S(2)}) copy-start(f32[1,32,64,128]{3,2,1,0:T(8,128)} %param.29) | copy-start | bytes 3145732
  95.0 13.3 %copy-start.8 = (f32[128,32,64]{0,2,1:T(8,128)S(1)}, f32[128,32,64]{0,2,1:T(8,128)}, u32[]{:S(2)}) copy-start(f32[128,32,64]{0,2,1:T(8,128)} %convolution_bitcast_fusion.1) | copy-start | bytes 3145732
  95.0 13.3 %copy-start.19 = (bf16[1,128,128]{2,1,0:T(8,128)(2,1)S(1)}, bf16[1,128,128]{2,1,0:T(8,128)(2,1)}, u32[]{:S(2)}) copy-start(bf16[1,128,128]{2,1,0:T(8,128)(2,1)} %param.25) | copy-start | bytes 98308
  95.1 13.3 %copy-start.21 = (f32[128,32]{0,1:T(8,128)S(1)}, f32[128,32]{0,1:T(8,128)}, u32[]{:S(2)}) copy-start(f32[128,32]{0,1:T(8,128)} %copy.123) | copy-start | bytes 49156
  95.1 13.3 %copy-start.26 = (f32[32]{0:T(128)S(1)}, f32[32]{0:T(128)}, u32[]{:S(2)}) copy-start(f32[32]{0:T(128)} %param.28) | copy-start | bytes 388
  97.0 8.6 %collective-permute-start.2 = (bf16[128,1024]{0,1:T(8,128)(2,1)S(1)}, bf16[128,1024]{0,1:T(8,128)(2,1)S(1)}, u32[]{:S(2)}, u32[]{:S(2)}) collective-permute-start(bf16[128,1024]{0,1:T(8,128)(2,1)S(1)} %collective-permute-done.1), channel_id=1, source_target_pairs={{0,1},{1,2},{2,3},{4,5},{5,6},{6,7},{8,9},{9,10},{10,11},{12,13},{... | collective-permute-start | bytes 786440 | tf_op jit(solution)/shard_map/ppermute | solution.py:21
  99.8 8.6 %collective-permute-start.8 = (bf16[32,64,128]{2,1,0:T(8,128)(2,1)S(1)}, bf16[32,64,128]{2,1,0:T(8,128)(2,1)S(1)}, u32[]{:S(2)}, u32[]{:S(2)}) collective-permute-start(bf16[32,64,128]{2,1,0:T(8,128)(2,1)S(1)} %add_convert_fusion), channel_id=1, source_target_pairs={{0,1},{1,2},{2,3},{4,5},{5,6},{6,7},{8,9},{9,10},{10,11},{12,13},{... | collective-permute-start | bytes 1572872 | tf_op jit(solution)/shard_map/ppermute | solution.py:21
  108.3 47.0 %copy-start.25 = (pred[1024]{0:T(1024)(128)(4,1)S(1)}, pred[1024]{0:T(1024)(128)(4,1)}, u32[]{:S(2)}) copy-start(pred[1024]{0:T(1024)(128)(4,1)} %lt.128) | copy-start | bytes 3076
  186.3 9.7 %copy-start.10 = (bf16[128,512]{0,1:T(8,128)(2,1)S(1)}, bf16[128,512]{0,1:T(8,128)(2,1)}, u32[]{:S(2)}) copy-start(bf16[128,512]{0,1:T(8,128)(2,1)} %get-tuple-element.222) | copy-start | bytes 393220
  (14 other events, 68.7 us)
where the time goes:
time: 201 us; the launch traced here: 199 us
  local copies, waits for them, and re-layouts  48.4 us (24%)
  waiting for transfers between devices  41.3 us (21%)
  starting transfers between devices  36.3 us (18%)
  matrix products  33.4 us (17%)
  other arithmetic  25 us (12%)
  blocking collectives  11.7 us (6%)
  between operations  2.51 us (1%)
    all_to_all x1, waiting for transfers between devices, fetch_pages(): lax.all_to_all(pool_pages[lax.all_to_all(wanted_slots, 'cache', split_axi...  40.6 us
    ppermute x9, starting transfers between devices, passed_along(): lax.ppermute(value, axis, [(source, source + steps) for source in range(l...  25.9 us
    scatter x1, local copies, waits for them, and re-layouts, fetch_pages(): jnp.zeros((owners_count, capacity), jnp.int32).at[owner_list, ranking]  19.7 us
    dot_general x6, matrix products, attend(): jnp.einsum('qhgd,khd->hgqk', grouped, keys_part, preferred_element_type=j...  17 us
    reduce_sum x6, other arithmetic, attend(): totals = totals * factor + jnp.sum(weights, axis=-1)  11.4 us
    dot_general x6, matrix products, attend(): jnp.einsum('hgqk,khd->hgqd', weights.astype(jnp.bfloat16), values_part, p...  10.5 us
    all_gather x1, blocking collectives, local(): lax.all_gather(page_owner[:, :, :, 0], 'blk', axis=1, tiled=True)  6.28 us
    unnamed x60, local copies, waits for them, and re-layouts  5.84 us
  transfers between devices with their start and end apart: 11, of which 2 were waited for; matrix products, arithmetic and copies ran while one was open for 18% of the time, Pallas kernels for 0%

commit v1 on v0

--- a/solution.py
+++ b/solution.py
@@ -1,3 +1,4 @@
+import functools
 import math
 import jax
 import jax.numpy as jnp
@@ -13,6 +14,37 @@
 PAGE = 8
 LIST = 32
 NEG = -1e30
+
+
+def serve_tables_here(inner_x, axis_k):
+    plain = list(inner_x.shape[1:])
+    plain[axis_k] *= inner_x.shape[0]
+    y_new = jnp.moveaxis(inner_x, 0, axis_k).reshape(plain)
+    return y_new
+
+
+def refer_lots_all_over_axis(inp, named_axis):
+    tall, b_now = (jax.lax.axis_size(named_axis), jax.lax.axis_index(named_axis))
+    then, main = (inp[None], 1)
+    while main < tall:
+        fields = []
+        for h in range(tall):
+            fields.append((h, h ^ main))
+        step_out = jax.lax.ppermute(then, axis_name=named_axis, perm=fields)
+        block_now = b_now & main == 0
+        then = jnp.concatenate(
+            [jnp.where(block_now, then, step_out), jnp.where(block_now, step_out, then)]
+        )
+        main *= 2
+    return then
+
+
+def manage_the_sample(x_part, vector, d_out):
+    row_out = serve_tables_here(refer_lots_all_over_axis(x_part, vector), d_out)
+    return row_out
+
+
+watch_domain_for = functools.partial(manage_the_sample, vector="blk", d_out=1)
 
 
 def passed_along(value, axis, steps):
@@ -110,7 +142,7 @@
     pool_pages = page_pool[0]
     capacity = max(2, 2 * LIST // lax.axis_size("cache"))
     all_owners, all_slots = (
-        lax.all_gather(page_owner[:, :, :, 0], "blk", axis=1, tiled=True),
+        watch_domain_for(page_owner[:, :, :, 0]),
         lax.all_gather(page_slot, "blk", axis=1, tiled=True),
     )
     fetched = fetch_pages(

time: 201 us -> 200 us (level)
  blocking collectives: 11.7 us -> 5.7 us
  starting transfers between devices: 36.3 us -> 40.2 us
    all_gather x1 -> x0, blocking collectives: 6.28 us -> none  [local(): lax.all_gather(page_owner[:, :, :, 0], 'blk', axis=1, tiled=True)]
    ppermute x0 -> x2, starting transfers between devices: none -> 3.17 us  [refer_lots_all_over_axis(): step_out = jax.lax.ppermute(then, axis_name=named_axis, perm=fields)]
    all_to_all x1, waiting for transfers between devices: 0.01 us -> 3.04 us  [fetch_pages(): lax.all_to_all(wanted_slots, 'cache', split_axis=0, concat_axis=0, tiled=...]
    all_to_all x1, waiting for transfers between devices: 40.6 us -> 37.9 us  [fetch_pages(): lax.all_to_all(pool_pages[lax.all_to_all(wanted_slots, 'cache', split_axi...]
  transfers between devices with their start and end apart: 11 -> 13, of which waited for: 2 -> 4; matrix products, arithmetic and copies ran while one was open for 18% -> 30% of each run, Pallas kernels for 0% -> 0%
where the time goes in v1:
time: 200 us; the launch traced here: 198 us
  local copies, waits for them, and re-layouts  48.5 us (24%)
  waiting for transfers between devices  41.7 us (21%)
  starting transfers between devices  40.2 us (20%)
  matrix products  33.4 us (17%)
  other arithmetic  26.4 us (13%)
  blocking collectives  5.7 us (3%)
  between operations  2.51 us (1%)
    all_to_all x1, waiting for transfers between devices, fetch_pages(): lax.all_to_all(pool_pages[lax.all_to_all(wanted_slots, 'cache', split_axi...  37.9 us
    ppermute x9, starting transfers between devices, passed_along(): lax.ppermute(value, axis, [(source, source + steps) for source in range(l...  27 us
    scatter x1, local copies, waits for them, and re-layouts, fetch_pages(): jnp.zeros((owners_count, capacity), jnp.int32).at[owner_list, ranking]  19.7 us
    dot_general x6, matrix products, attend(): jnp.einsum('qhgd,khd->hgqk', grouped, keys_part, preferred_element_type=j...  16.9 us
    reduce_sum x6, other arithmetic, attend(): totals = totals * factor + jnp.sum(weights, axis=-1)  11.9 us
    dot_general x6, matrix products, attend(): jnp.einsum('hgqk,khd->hgqd', weights.astype(jnp.bfloat16), values_part, p...  10.6 us
    unnamed x60, local copies, waits for them, and re-layouts  5.94 us
    all_gather x1, blocking collectives, local(): lax.all_gather(page_slot, 'blk', axis=1, tiled=True)  5.7 us
  transfers between devices with their start and end apart: 13, of which 4 were waited for; matrix products, arithmetic and copies ran while one was open for 30% of the time, Pallas kernels for 0%

profile of v1, /device:TPU:0, one launch (start us, length us, event | category | flops | bytes accessed | tf_op | source)
XLA Modules:
  0.0 198.4 jit_solution(1327305746925759992)
XLA Ops:
  2.4 2.7 %collective-permute-start.2 = (bf16[128,1024]{0,1:T(8,128)(2,1)S(1)}, bf16[128,1024]{0,1:T(8,128)(2,1)}, u32[]{:S(2)}, u32[]{:S(2)}) collective-permute-start(bf16[128,1024]{0,1:T(8,128)(2,1)S(1)} %bitcast.244), channel_id=1, source_target_pairs={{0,1},{1,2},{2,3},{4,5},{5,6},{6,7},{8,9},{9,10},{10,11},{12,13},{... | collective-permute-start | bytes 786440 | tf_op jit(solution)/shard_map/ppermute | solution.py:53
  5.1 5.7 %all_gather.3 = s32[1,4,32]{2,0,1:T(1,128)S(1)} all-gather(s32[1,1,32]{2,0,1:T(1,128)} %bitcast.280), channel_id=1, replica_groups=mesh['groups'=2,'cache'=4,'blk'=4] {'blk'}, dimensions={1}, use_global_device_ids=true | all-gather | bytes 640 | tf_op jit(solution)/shard_map/all_gather | solution.py:146
  12.9 2.7 %collective-permute-start.1 = (s32[2,1,1,32]{3,2,1,0:T(1,128)S(1)}, s32[2,1,1,32]{3,2,1,0:T(1,128)S(1)}, u32[]{:S(2)}, u32[]{:S(2)}) collective-permute-start(s32[2,1,1,32]{3,2,1,0:T(1,128)S(1)} %pad_add_fusion.1), channel_id=1, source_target_pairs={{0,2},{1,3},{2,0},{3,1},{4,6},{5,7},{6,4},{7,5},{8,10},{9,11},{10,... | collective-permute-start | bytes 776 | tf_op jit(solution)/shard_map/ppermute | solution.py:33
  19.0 19.7 %scatter_fusion = s32[4,64]{1,0:T(4,128)} fusion(s32[4,64]{1,0:T(4,128)} %broadcast.351, s32[128]{0:T(128)S(1)} %get-tuple-element.209, s32[128]{0:T(128)S(1)} %reshape.502), kind=kCustom, calls=%fused_computation.2 | custom fusion | bytes 2560 | tf_op jit(solution)/shard_map/scatter | solution.py:95
  38.7 5.0 %all-to-all-start = ((s32[4,1,64]{2,1,0:T(1,128)}), s32[4,1,64]{2,1,0:T(1,128)S(1)}, u32[]{:S(2)}, u32[]{:S(2)}) async-start(s32[4,1,64]{2,1,0:T(1,128)} %bitcast.8), calls=%async_computation | async-start | bytes 4096 | tf_op jit(solution)/shard_map/all_to_all | solution.py:98
  46.2 3.0 %all-to-all-done = s32[4,1,64]{2,1,0:T(1,128)S(1)} async-done(((s32[4,1,64]{2,1,0:T(1,128)}), s32[4,1,64]{2,1,0:T(1,128)S(1)}, u32[]{:S(2)}, u32[]{:S(2)}) %all-to-all-start) | async-done | bytes 1056 | tf_op jit(solution)/shard_map/all_to_all | solution.py:98
  49.3 2.8 %gather_fusion = bf16[256,8,1024]{2,1,0:T(8,128)(2,1)} fusion(bf16[128,8,1024]{2,1,0:T(8,128)(2,1)S(1)} %bitcast.227, s32[1024]{0:T(1024)S(1)} %pad_clamp_fusion), kind=kCustom, calls=%fused_computation | custom fusion | bytes 8389632 | tf_op jit(solution)/shard_map/gather | solution.py:98
  52.1 5.0 %all-to-all-start.1 = ((bf16[4,64,8,1024]{3,2,1,0:T(8,128)(2,1)}), bf16[4,64,8,1024]{3,2,1,0:T(8,128)(2,1)}, u32[]{:S(2)}, u32[]{:S(2)}) async-start(bf16[4,64,8,1024]{3,2,1,0:T(8,128)(2,1)} %bitcast.235), calls=%async_computation.1 | async-start | bytes 8388608 | tf_op jit(solution)/shard_map/all_to_all | solution.py:97
  65.1 2.7 %convolution_bitcast_fusion.1 = f32[128,32,64]{0,2,1:T(8,128)} fusion(bf16[128,32,64]{0,2,1:T(8,128)(2,1)S(1)} %bitcast.238, f32[32,128]{1,0:T(8,128)} %bitcast.276, f32[32,128]{1,0:T(8,128)} %copy.118, f32[128,128]{1,0:T(8,128)S(1)} %fusion.73, pred[128,128]{1,0:T(8,128)(4,1)S(1)} %iota_compare_fusion), kind=kOutput, calls=%fused_computation.46 | convolution fusion | flops 69730304 | bytes 1687552 | tf_op jit(solution)/shard_map/hts,shp->thp/dot_general | solution.py:194
  74.9 5.2 %collective-permute-start.8 = (bf16[32,64,128]{2,1,0:T(8,128)(2,1)}, bf16[32,64,128]{2,1,0:T(8,128)(2,1)}, u32[]{:S(2)}, u32[]{:S(2)}) collective-permute-start(bf16[32,64,128]{2,1,0:T(8,128)(2,1)} %get-tuple-element.246), channel_id=1, source_target_pairs={{0,1},{1,2},{2,3},{4,5},{5,6},{6,7},{8,9},{9,10},{10,11},{12,13},{... | collective-permute-start | bytes 1572872 | tf_op jit(solution)/shard_map/ppermute | solution.py:53
  81.9 3.4 %collective-permute-start.7 = (bf16[32]{0:T(256)(128)(2,1)S(1)}, bf16[32]{0:T(256)(128)(2,1)S(1)}, u32[]{:S(2)}, u32[]{:S(2)}) collective-permute-start(bf16[32]{0:T(256)(128)(2,1)S(1)} %get-tuple-element.227), channel_id=1, source_target_pairs={{0,1},{1,2},{2,3},{4,5},{5,6},{6,7},{8,9},{9,10},{10,11},{12,13},{... | collective-permute-start | bytes 200 | tf_op jit(solution)/shard_map/ppermute | solution.py:53
  86.8 3.1 %collective-permute-start.3 = (bf16[128,1024]{0,1:T(8,128)(2,1)}, bf16[128,1024]{0,1:T(8,128)(2,1)S(1)}, u32[]{:S(2)}, u32[]{:S(2)}) collective-permute-start(bf16[128,1024]{0,1:T(8,128)(2,1)} %collective-permute-done.2), channel_id=1, source_target_pairs={{0,1},{1,2},{2,3},{4,5},{5,6},{6,7},{8,9},{9,10},{10,11},{12,13},{... | collective-permute-start | bytes 786440 | tf_op jit(solution)/shard_map/ppermute | solution.py:53
  91.5 4.4 %collective-permute-start.9 = (bf16[32,64,128]{2,1,0:T(8,128)(2,1)S(1)}, bf16[32,64,128]{2,1,0:T(8,128)(2,1)S(1)}, u32[]{:S(2)}, u32[]{:S(2)}) collective-permute-start(bf16[32,64,128]{2,1,0:T(8,128)(2,1)S(1)} %add_convert_fusion.1), channel_id=1, source_target_pairs={{0,1},{1,2},{2,3},{4,5},{5,6},{6,7},{8,9},{9,10},{10,11},{12,13},{... | collective-permute-start | bytes 1572872 | tf_op jit(solution)/shard_map/ppermute | solution.py:53
  101.7 3.2 %collective-permute-start.10 = (bf16[32,64,128]{2,1,0:T(8,128)(2,1)S(1)}, bf16[32,64,128]{2,1,0:T(8,128)(2,1)S(1)}, u32[]{:S(2)}, u32[]{:S(2)}) collective-permute-start(bf16[32,64,128]{2,1,0:T(8,128)(2,1)S(1)} %add_convert_fusion), channel_id=1, source_target_pairs={{0,1},{1,2},{2,3},{4,5},{5,6},{6,7},{8,9},{9,10},{10,11},{12,13},{... | collective-permute-start | bytes 1572872 | tf_op jit(solution)/shard_map/ppermute | solution.py:53
  112.2 37.9 %all-to-all-done.1 = bf16[4,64,8,1024]{3,2,1,0:T(8,128)(2,1)} async-done(((bf16[4,64,8,1024]{3,2,1,0:T(8,128)(2,1)}), bf16[4,64,8,1024]{3,2,1,0:T(8,128)(2,1)}, u32[]{:S(2)}, u32[]{:S(2)}) %all-to-all-start.1) | async-done | bytes 4194336 | tf_op jit(solution)/shard_map/all_to_all | solution.py:97
  150.1 4.4 %gather_fusion.1 = bf16[128,8,1024]{2,1,0:T(8,128)(2,1)} fusion(bf16[4,64,8,1024]{3,2,1,0:T(8,128)(2,1)} %all-to-all-done.1, s32[128]{0:T(128)S(1)} %bitcast.237), kind=kCustom, calls=%fused_computation.1 | custom fusion | bytes 4195328 | tf_op jit(solution)/shard_map/gather | solution.py:104
  154.5 31.0 %while.18 = (s32[]{:T(128)}, f32[4,4,128]{2,1,0:T(4,128)S(1)}, f32[4,4,128]{2,1,0:T(4,128)}, f32[4,4,128,128]{3,2,1,0:T(8,128)}, pred[1024]{0:T(1024)(128)(4,1)S...) while((s32[]{:T(128)}, f32[4,4,128]{2,1,0:T(4,128)S(1)}, ...), condition=%wide.region_6.7_spmd.clone, body=%wide.region_3.6_spmd.clone.sunk | while | flops 549201920 | bytes 20581064 | solution.py:165
  156.9 4.2 %fusion.130 = (f32[4,4,128]{2,1,0:T(4,128)S(1)}, f32[4,512,128,4]{2,1,3,0:T(8,128)}) fusion(pred[512]{0:T(512)(128)(4,1)S(1)} %dynamic_slice.17, bf16[512,4,128,1]{0,2,3,1:T(8,128)(2,1)} %bitcast.228, bf16[128,4,4,128]{3,0,2,1:T(8,128)(2,1)} %get-tuple-element.350), kind=kOutput, calls=%fused_computation.5.clone.1 | convolution fusion | flops 271579136 | bytes 5251584 | tf_op jit(solution)/shard_map/while/body/eval_jaxpr/qhgd,khd->hgqk/dot_general | solution.py:70
  161.1 3.1 %fusion.131 = f32[4,4,128]{2,1,0:T(4,128)S(1)} fusion(f32[4,512,128,4]{2,1,3,0:T(8,128)} %get-tuple-element.316, f32[4,4,128]{2,1,0:T(4,128)S(1)} %select_maximum_fusion.2, pred[512]{0:T(512)(128)(4,1)S(1)} %dynamic_slice.17), kind=kLoop, calls=%fused_computation.9.clone.1 | loop fusion | flops 4192256 | bytes 4211200 | tf_op jit(solution)/shard_map/while/body/eval_jaxpr/reduce_sum | solution.py:77
  165.0 4.5 %fusion.133 = f32[4,4,128,128]{3,2,1,0:T(8,128)} fusion(bf16[512,4,128,1]{0,2,3,1:T(8,128)(2,1)S(1)} %bitcast.236, f32[4,512,128,4]{2,1,3,0:T(8,128)} %get-tuple-element.316, f32[4,4,128]{2,1,0:T(4,128)S(1)} %select_maximum_fusion.2, pred[512]{0:T(512)(128)(4,1)S(1)} %dynamic_slice.17, f32[4,4,128,128]{3,2,1,0:T(8,128)} %get-tuple-element.335, ...), kind=kOutput, calls=%fused_computation.15.clone.1 | convolution fusion | flops 273416192 | bytes 6832641 | tf_op jit(solution)/shard_map/while/body/eval_jaxpr/hgqk,khd->hgqd/dot_general | solution.py:78
  171.9 4.2 %fusion.130 = (f32[4,4,128]{2,1,0:T(4,128)S(1)}, f32[4,512,128,4]{2,1,3,0:T(8,128)}) fusion(pred[512]{0:T(512)(128)(4,1)S(1)} %dynamic_slice.17, bf16[512,4,128,1]{0,2,3,1:T(8,128)(2,1)} %bitcast.228, bf16[128,4,4,128]{3,0,2,1:T(8,128)(2,1)} %get-tuple-element.350), kind=kOutput, calls=%fused_computation.5.clone.1 | convolution fusion | flops 271579136 | bytes 5251584 | tf_op jit(solution)/shard_map/while/body/eval_jaxpr/qhgd,khd->hgqk/dot_general | solution.py:70
  176.1 3.1 %fusion.131 = f32[4,4,128]{2,1,0:T(4,128)S(1)} fusion(f32[4,512,128,4]{2,1,3,0:T(8,128)} %get-tuple-element.316, f32[4,4,128]{2,1,0:T(4,128)S(1)} %select_maximum_fusion.2, pred[512]{0:T(512)(128)(4,1)S(1)} %dynamic_slice.17), kind=kLoop, calls=%fused_computation.9.clone.1 | loop fusion | flops 4192256 | bytes 4211200 | tf_op jit(solution)/shard_map/while/body/eval_jaxpr/reduce_sum | solution.py:77
  180.7 4.8 %fusion.133 = f32[4,4,128,128]{3,2,1,0:T(8,128)} fusion(bf16[512,4,128,1]{0,2,3,1:T(8,128)(2,1)S(1)} %bitcast.236, f32[4,512,128,4]{2,1,3,0:T(8,128)} %get-tuple-element.316, f32[4,4,128]{2,1,0:T(4,128)S(1)} %select_maximum_fusion.2, pred[512]{0:T(512)(128)(4,1)S(1)} %dynamic_slice.17, f32[4,4,128,128]{3,2,1,0:T(8,128)} %get-tuple-element.335, ...), kind=kOutput, calls=%fused_computation.15.clone.1 | convolution fusion | flops 273416192 | bytes 6832641 | tf_op jit(solution)/shard_map/while/body/eval_jaxpr/hgqk,khd->hgqd/dot_general | solution.py:78
  185.5 2.7 %copy.105 = f32[4,4,128,128]{2,3,1,0:T(8,128)} copy(f32[4,4,128,128]{3,2,1,0:T(8,128)} %get-tuple-element.128) | data formatting | bytes 2097152 | tf_op jit(solution)/shard_map/while | solution.py:165
  (158 shorter events, 58.5 us)
Async XLA Ops:
  0.6 48.7 %copy-start = (bf16[1,128,8,1024]{3,2,1,0:T(8,128)(2,1)S(1)}, bf16[1,128,8,1024]{3,2,1,0:T(8,128)(2,1)}, u32[]{:S(2)}) copy-start(bf16[1,128,8,1024]{3,2,1,0:T(8,128)(2,1)} %param.18) | copy-start | bytes 6291460
  0.6 11.6 %collective-permute-start = (s32[1,1,1,32]{3,2,1,0:T(1,128)}, s32[1,1,1,32]{3,2,1,0:T(1,128)S(1)}, u32[]{:S(2)}, u32[]{:S(2)}) collective-permute-start(s32[1,1,1,32]{3,2,1,0:T(1,128)} %bitcast.281), channel_id=1, source_target_pairs={{0,1},{1,0},{2,3},{3,2},{4,5},{5,4},{6,7},{7,6},{8,9},{9,8},{10,11... | collective-permute-start | bytes 392 | tf_op jit(solution)/shard_map/ppermute | solution.py:33
  2.4 84.4 %collective-permute-start.2 = (bf16[128,1024]{0,1:T(8,128)(2,1)S(1)}, bf16[128,1024]{0,1:T(8,128)(2,1)}, u32[]{:S(2)}, u32[]{:S(2)}) collective-permute-start(bf16[128,1024]{0,1:T(8,128)(2,1)S(1)} %bitcast.244), channel_id=1, source_target_pairs={{0,1},{1,2},{2,3},{4,5},{5,6},{6,7},{8,9},{9,10},{10,11},{12,13},{... | collective-permute-start | bytes 786440 | tf_op jit(solution)/shard_map/ppermute | solution.py:53
  12.9 4.2 %collective-permute-start.1 = (s32[2,1,1,32]{3,2,1,0:T(1,128)S(1)}, s32[2,1,1,32]{3,2,1,0:T(1,128)S(1)}, u32[]{:S(2)}, u32[]{:S(2)}) collective-permute-start(s32[2,1,1,32]{3,2,1,0:T(1,128)S(1)} %pad_add_fusion.1), channel_id=1, source_target_pairs={{0,2},{1,3},{2,0},{3,1},{4,6},{5,7},{6,4},{7,5},{8,10},{9,11},{10,... | collective-permute-start | bytes 776 | tf_op jit(solution)/shard_map/ppermute | solution.py:33
  38.7 10.5 %all-to-all-start = ((s32[4,1,64]{2,1,0:T(1,128)}), s32[4,1,64]{2,1,0:T(1,128)S(1)}, u32[]{:S(2)}, u32[]{:S(2)}) async-start(s32[4,1,64]{2,1,0:T(1,128)} %bitcast.8), calls=%async_computation | async-start | bytes 4096 | tf_op jit(solution)/shard_map/all_to_all | solution.py:98
  44.3 26.4 %collective-permute-start.5 = (bf16[32]{0:T(256)(128)(2,1)}, bf16[32]{0:T(256)(128)(2,1)}, u32[]{:S(2)}, u32[]{:S(2)}) collective-permute-start(bf16[32]{0:T(256)(128)(2,1)} %fusion.89), channel_id=1, source_target_pairs={{0,1},{1,2},{2,3},{4,5},{5,6},{6,7},{8,9},{9,10},{10,11},{12,13},{... | collective-permute-start | bytes 200 | tf_op jit(solution)/shard_map/ppermute | solution.py:53
  52.1 98.0 %all-to-all-start.1 = ((bf16[4,64,8,1024]{3,2,1,0:T(8,128)(2,1)}), bf16[4,64,8,1024]{3,2,1,0:T(8,128)(2,1)}, u32[]{:S(2)}, u32[]{:S(2)}) async-start(bf16[4,64,8,1024]{3,2,1,0:T(8,128)(2,1)} %bitcast.235), calls=%async_computation.1 | async-start | bytes 8388608 | tf_op jit(solution)/shard_map/all_to_all | solution.py:97
  67.8 29.2 %copy-start.12 = (pred[128,128]{0,1:T(8,128)(4,1)S(1)}, pred[128,128]{0,1:T(8,128)(4,1)}, u32[]{:S(2)}) copy-start(pred[128,128]{0,1:T(8,128)(4,1)} %get-tuple-element.237) | copy-start | bytes 49156
  71.4 2.1 %collective-permute-start.6 = (bf16[32]{0:T(256)(128)(2,1)S(1)}, bf16[32]{0:T(256)(128)(2,1)S(1)}, u32[]{:S(2)}, u32[]{:S(2)}) collective-permute-start(bf16[32]{0:T(256)(128)(2,1)S(1)} %fusion.78), channel_id=1, source_target_pairs={{0,1},{1,2},{2,3},{4,5},{5,6},{6,7},{8,9},{9,10},{10,11},{12,13},{... | collective-permute-start | bytes 200 | tf_op jit(solution)/shard_map/ppermute | solution.py:53
  73.5 25.4 %copy-start.22 = (f32[32]{0:T(128)}, f32[32]{0:T(128)S(1)}, u32[]{:S(2)}) copy-start(f32[32]{0:T(128)S(1)} %get-tuple-element.229) | copy-start | bytes 388
  74.9 15.0 %collective-permute-start.8 = (bf16[32,64,128]{2,1,0:T(8,128)(2,1)}, bf16[32,64,128]{2,1,0:T(8,128)(2,1)}, u32[]{:S(2)}, u32[]{:S(2)}) collective-permute-start(bf16[32,64,128]{2,1,0:T(8,128)(2,1)} %get-tuple-element.246), channel_id=1, source_target_pairs={{0,1},{1,2},{2,3},{4,5},{5,6},{6,7},{8,9},{9,10},{10,11},{12,13},{... | collective-permute-start | bytes 1572872 | tf_op jit(solution)/shard_map/ppermute | solution.py:53
  80.2 30.1 %copy-start.23 = (pred[128]{0:T(512)(128)(4,1)}, pred[128]{0:T(512)(128)(4,1)S(1)}, u32[]{:S(2)}) copy-start(pred[128]{0:T(512)(128)(4,1)S(1)} %broadcast_compare_fusion.4) | copy-start | bytes 388
  81.9 4.9 %collective-permute-start.7 = (bf16[32]{0:T(256)(128)(2,1)S(1)}, bf16[32]{0:T(256)(128)(2,1)S(1)}, u32[]{:S(2)}, u32[]{:S(2)}) collective-permute-start(bf16[32]{0:T(256)(128)(2,1)S(1)} %get-tuple-element.227), channel_id=1, source_target_pairs={{0,1},{1,2},{2,3},{4,5},{5,6},{6,7},{8,9},{9,10},{10,11},{12,13},{... | collective-permute-start | bytes 200 | tf_op jit(solution)/shard_map/ppermute | solution.py:53
  86.7 14.1 %copy-start.4 = (f32[32,64,128]{2,1,0:T(8,128)S(1)}, f32[32,64,128]{2,1,0:T(8,128)}, u32[]{:S(2)}) copy-start(f32[32,64,128]{2,1,0:T(8,128)} %get-tuple-element.247) | copy-start | bytes 3145732
  86.8 12.2 %collective-permute-start.3 = (bf16[128,1024]{0,1:T(8,128)(2,1)}, bf16[128,1024]{0,1:T(8,128)(2,1)S(1)}, u32[]{:S(2)}, u32[]{:S(2)}) collective-permute-start(bf16[128,1024]{0,1:T(8,128)(2,1)} %collective-permute-done.2), channel_id=1, source_target_pairs={{0,1},{1,2},{2,3},{4,5},{5,6},{6,7},{8,9},{9,10},{10,11},{12,13},{... | collective-permute-start | bytes 786440 | tf_op jit(solution)/shard_map/ppermute | solution.py:53
  89.9 18.4 %copy-start.16 = (pred[128,128]{0,1:T(8,128)(4,1)S(1)}, pred[128,128]{0,1:T(8,128)(4,1)}, u32[]{:S(2)}) copy-start(pred[128,128]{0,1:T(8,128)(4,1)} %get-tuple-element.236) | copy-start | bytes 49156
  91.5 9.4 %collective-permute-start.9 = (bf16[32,64,128]{2,1,0:T(8,128)(2,1)S(1)}, bf16[32,64,128]{2,1,0:T(8,128)(2,1)S(1)}, u32[]{:S(2)}, u32[]{:S(2)}) collective-permute-start(bf16[32,64,128]{2,1,0:T(8,128)(2,1)S(1)} %add_convert_fusion.1), channel_id=1, source_target_pairs={{0,1},{1,2},{2,3},{4,5},{5,6},{6,7},{8,9},{9,10},{10,11},{12,13},{... | collective-permute-start | bytes 1572872 | tf_op jit(solution)/shard_map/ppermute | solution.py:53
  96.9 13.4 %copy-start.7 = (f32[1,32,64,128]{3,2,1,0:T(8,128)S(1)}, f32[1,32,64,128]{3,2,1,0:T(8,128)}, u32[]{:S(2)}) copy-start(f32[1,32,64,128]{3,2,1,0:T(8,128)} %param.29) | copy-start | bytes 3145732
  96.9 13.4 %copy-start.8 = (f32[128,32,64]{0,2,1:T(8,128)S(1)}, f32[128,32,64]{0,2,1:T(8,128)}, u32[]{:S(2)}) copy-start(f32[128,32,64]{0,2,1:T(8,128)} %convolution_bitcast_fusion.1) | copy-start | bytes 3145732
  96.9 13.4 %copy-start.19 = (bf16[1,128,128]{2,1,0:T(8,128)(2,1)S(1)}, bf16[1,128,128]{2,1,0:T(8,128)(2,1)}, u32[]{:S(2)}) copy-start(bf16[1,128,128]{2,1,0:T(8,128)(2,1)} %param.25) | copy-start | bytes 98308
  96.9 13.3 %copy-start.21 = (f32[128,32]{0,1:T(8,128)S(1)}, f32[128,32]{0,1:T(8,128)}, u32[]{:S(2)}) copy-start(f32[128,32]{0,1:T(8,128)} %copy.122) | copy-start | bytes 49156
  98.9 8.7 %collective-permute-start.4 = (bf16[128,1024]{0,1:T(8,128)(2,1)S(1)}, bf16[128,1024]{0,1:T(8,128)(2,1)S(1)}, u32[]{:S(2)}, u32[]{:S(2)}) collective-permute-start(bf16[128,1024]{0,1:T(8,128)(2,1)S(1)} %collective-permute-done.3), channel_id=1, source_target_pairs={{0,1},{1,2},{2,3},{4,5},{5,6},{6,7},{8,9},{9,10},{10,11},{12,13},{... | collective-permute-start | bytes 786440 | tf_op jit(solution)/shard_map/ppermute | solution.py:53
  101.7 8.5 %collective-permute-start.10 = (bf16[32,64,128]{2,1,0:T(8,128)(2,1)S(1)}, bf16[32,64,128]{2,1,0:T(8,128)(2,1)S(1)}, u32[]{:S(2)}, u32[]{:S(2)}) collective-permute-start(bf16[32,64,128]{2,1,0:T(8,128)(2,1)S(1)} %add_convert_fusion), channel_id=1, source_target_pairs={{0,1},{1,2},{2,3},{4,5},{5,6},{6,7},{8,9},{9,10},{10,11},{12,13},{... | collective-permute-start | bytes 1572872 | tf_op jit(solution)/shard_map/ppermute | solution.py:53
  110.3 44.2 %copy-start.25 = (pred[1024]{0:T(1024)(128)(4,1)S(1)}, pred[1024]{0:T(1024)(128)(4,1)}, u32[]{:S(2)}) copy-start(pred[1024]{0:T(1024)(128)(4,1)} %lt.128) | copy-start | bytes 3076
  (16 other events, 96.7 us)
